TPU v7x, 512 devices: a whole 4x8x8 slice. The times are simulated.
512 devices in a mesh: dp: 4 (over x), row: 16 (over y, core), col: 8 (over z).
Axes of the slice: x: 4, y: 8, z: 8, core: 2. Of those that a mesh axis runs over, the one named last changes fastest.
Arguments:
- grad_wi: bfloat16 [4, 4096, 16384], P('dp', 'row', 'col'), may hold values from -100 to 100
- grad_wo: bfloat16 [4, 16384, 4096], P('dp', 'row', 'col'), may hold values from -100 to 100
- row_wi: float32 [4096], P('row'), may hold values from 0.01 to 1
- col_wi: float32 [16384], P('col'), may hold values from 0.01 to 1
- row_wo: float32 [16384], P('row'), may hold values from 0.01 to 1
- col_wo: float32 [4096], P('col'), may hold values from 0.01 to 1
Outputs:
- update_wi: bfloat16 [4096, 16384], P('row', 'col')
- row_wi_new: float32 [4096], P('row')
- col_wi_new: float32 [16384], P('col')
- update_wo: bfloat16 [16384, 4096], P('row', 'col')
- row_wo_new: float32 [16384], P('row')
- col_wo_new: float32 [4096], P('col')
All inputs are finite; a program needn't handle non-finite values.
Results may differ from a plain program's by a relative error of at most 0.015.
Values may be sent and summed in bfloat16 or wider, within the bound.
A program may use at most 64 MiB of HBM per device.

v0:
```python
import jax
import jax.numpy as jnp
from jax import lax
from jax.sharding import PartitionSpec as P

D = 4096
FF = 16384
BETA = 0.8
EPS_SQUARE = 1e-30


def column_totals(square_wi, square_wo):
    return lax.psum((jnp.sum(square_wi, axis=0), jnp.sum(square_wo, axis=0)), "row")


def local(grad_wi, grad_wo, row_wi, col_wi, row_wo, col_wo):
    terms = (grad_wi[0].astype(jnp.float32), grad_wo[0].astype(jnp.float32))
    total_wi, total_wo = (
        lax.psum(terms[0].astype(jnp.bfloat16), "dp").astype(jnp.float32),
        lax.psum(terms[1].astype(jnp.bfloat16), "dp").astype(jnp.float32),
    )
    square_wi = total_wi * total_wi + EPS_SQUARE
    square_wo = total_wo * total_wo + EPS_SQUARE
    row_sum_wi, row_sum_wo = lax.psum(
        (jnp.sum(square_wi, axis=1), jnp.sum(square_wo, axis=1)), "col"
    )
    col_sum_wi, col_sum_wo = column_totals(square_wi, square_wo)
    row_new_wi = BETA * row_wi + (1.0 - BETA) * (row_sum_wi / FF)
    row_new_wo = BETA * row_wo + (1.0 - BETA) * (row_sum_wo / D)
    col_new_wi = BETA * col_wi + (1.0 - BETA) * (col_sum_wi / D)
    col_new_wo = BETA * col_wo + (1.0 - BETA) * (col_sum_wo / FF)
    raw_wi = total_wi / jnp.sqrt(row_new_wi[:, None] * col_new_wi[None, :])
    raw_wo = total_wo / jnp.sqrt(row_new_wo[:, None] * col_new_wo[None, :])
    local_squares = (jnp.sum(raw_wi * raw_wi), jnp.sum(raw_wo * raw_wo))
    energy_wi, energy_wo = lax.psum((local_squares[0], local_squares[1]), ("row", "col"))
    update_wi = (raw_wi / jnp.maximum(1.0, jnp.sqrt(energy_wi / (D * FF)))).astype(jnp.bfloat16)
    update_wo = (raw_wo / jnp.maximum(1.0, jnp.sqrt(energy_wo / (D * FF)))).astype(jnp.bfloat16)
    return (update_wi, row_new_wi, col_new_wi, update_wo, row_new_wo, col_new_wo)


def solution(mesh):
    return jax.shard_map(
        local,
        mesh=mesh,
        in_specs=(
            P("dp", "row", "col"),
            P("dp", "row", "col"),
            P("row"),
            P("col"),
            P("row"),
            P("col"),
        ),
        out_specs=(P("row", "col"), P("row"), P("col"), P("row", "col"), P("row"), P("col")),
        check_vma=False,
    )
```

profile of v0, /device:TPU:64, one launch (start us, length us, event | category | flops | bytes accessed | tf_op | source)
XLA Modules:
  0.0 412.7 jit_solution(8415651941492895730)
XLA Ops:
  7.2 0.0 all-reduce.6.cloned.1.call-start
  7.2 0.7 all-reduce.6.cloned.1.call-update
  7.9 76.1 %all-reduce.6.cloned.1.call-done = (bf16[256,2048]{1,0:T(8,128)(2,1)}, bf16[1024,512]{1,0:T(8,128)(2,1)}) async-done(((bf16[256,2048]{1,0:T(8,128)(2,1)}, bf16[1024,512]{1,0:T(8,128)(2,1)}), (bf16[256,2048]{1,0:T(8,128)(2,1)}, bf16[1024,512]{1,0:T(8,128)(2,1)})) %all-reduce.6.cloned.1.call-update) | async-done | bytes 2097168 | tf_op jit(solution)/shard_map/psum | solution.py:19
  84.0 1.8 fusion.5
  85.8 0.0 copy-done.1
  85.8 0.0 copy-start.8
  85.8 0.0 copy-start
  85.8 0.5 fusion.2
  86.3 16.8 %all-reduce.2 = (f32[256]{0:T(256)S(1)}, f32[1024]{0:T(1024)S(1)}) all-reduce(f32[256]{0:T(256)S(1)} %get-tuple-element.8, f32[1024]{0:T(1024)S(1)} %get-tuple-element.6), channel_id=1, replica_groups=mesh['dp'=4,'row'=16,'col'=8] {'col'}, use_global_device_ids=true, to_apply=%region_2.0 | all-reduce | flops 1280 | bytes 10240 | tf_op jit(solution)/shard_map/psum | solution.py:24
  103.1 0.0 copy-done.9
  103.1 0.0 copy-start.5
  103.1 0.0 copy-done.7
  103.1 0.0 copy-start.3
  103.2 45.7 %all-reduce.1 = (f32[2048]{0:T(1024)S(1)}, f32[512]{0:T(512)S(1)}) all-reduce(f32[2048]{0:T(1024)S(1)} %get-tuple-element.9, f32[512]{0:T(512)S(1)} %get-tuple-element.7), channel_id=1, replica_groups=mesh['dp'=4,'row'=16,'col'=8] {'row'}, use_global_device_ids=true, to_apply=%region_4.0 | all-reduce | flops 2560 | bytes 20480 | tf_op jit(solution)/shard_map/psum | solution.py:13
  148.9 0.0 copy-done.6
  148.9 1.5 multiply_reduce_fusion.1
  150.4 0.0 copy-done.8
  150.4 0.0 copy-done
  150.4 0.0 copy-start.4
  150.4 1.4 multiply_reduce_fusion
  151.9 249.7 %all-reduce = (f32[]{:T(128)}, f32[]{:T(128)}) all-reduce(f32[]{:T(128)} %multiply_reduce_fusion.1, f32[]{:T(128)} %multiply_reduce_fusion), channel_id=1, replica_groups=mesh['dp'=4,'row'=16,'col'=8] {'row','col'}, use_global_device_ids=true, to_apply=%region_6.0 | all-reduce | flops 2 | bytes 16 | tf_op jit(solution)/shard_map/psum | solution.py:35
  403.0 0.0 copy-done.5
  403.0 1.4 divide_convert_fusion.1
  404.4 1.4 divide_convert_fusion
  (12 shorter events, 0.0 us)
Async XLA Ops:
  7.2 76.8 %all-reduce.6.cloned.1.call-start = ((), (), s32[]{:S(2)}) async-start(), calls=%async_computation | async-start | bytes 4194304 | tf_op jit(solution)/shard_map/psum | solution.py:19
  84.0 1.8 copy-start.1
  84.0 19.1 %copy-start.9 = (f32[256]{0:T(256)S(1)}, f32[256]{0:T(256)}, u32[]{:S(2)}) copy-start(f32[256]{0:T(256)} %param.8) | copy-start | bytes 3076
  84.0 19.1 %copy-start.7 = (f32[1024]{0:T(1024)S(1)}, f32[1024]{0:T(1024)}, u32[]{:S(2)}) copy-start(f32[1024]{0:T(1024)} %param.10) | copy-start | bytes 12292
  84.0 64.9 %copy-start.6 = (f32[2048]{0:T(1024)S(1)}, f32[2048]{0:T(1024)}, u32[]{:S(2)}) copy-start(f32[2048]{0:T(1024)} %param.9) | copy-start | bytes 24580
  85.8 64.6 %copy-start.8 = (f32[512]{0:T(512)S(1)}, f32[512]{0:T(512)}, u32[]{:S(2)}) copy-start(f32[512]{0:T(512)} %param.11) | copy-start | bytes 6148
  85.8 64.6 %copy-start = (bf16[1024,512]{1,0:T(8,128)(2,1)S(1)}, bf16[1024,512]{1,0:T(8,128)(2,1)}, u32[]{:S(2)}) copy-start(bf16[1024,512]{1,0:T(8,128)(2,1)} %get-tuple-element.17) | copy-start | bytes 3145732
  103.1 299.9 %copy-start.5 = (f32[256]{0:T(256)}, f32[256]{0:T(256)S(1)}, u32[]{:S(2)}) copy-start(f32[256]{0:T(256)S(1)} %multiply_add_fusion.3) | copy-start | bytes 3076
  103.1 301.3 %copy-start.3 = (f32[1024]{0:T(1024)}, f32[1024]{0:T(1024)S(1)}, u32[]{:S(2)}) copy-start(f32[1024]{0:T(1024)S(1)} %multiply_add_fusion.1) | copy-start | bytes 12292
  148.9 254.1 %copy-start.2 = (f32[2048]{0:T(1024)}, f32[2048]{0:T(1024)S(1)}, u32[]{:S(2)}) copy-start(f32[2048]{0:T(1024)S(1)} %multiply_add_fusion) | copy-start | bytes 24580
  150.4 254.0 %copy-start.4 = (f32[512]{0:T(512)}, f32[512]{0:T(512)S(1)}, u32[]{:S(2)}) copy-start(f32[512]{0:T(512)S(1)} %multiply_add_fusion.2) | copy-start | bytes 6148
Sparse Core Ops, SparseCore 0:
  10.4 73.4 all-reduce.5
where the time goes:
time: 413 us
  blocking collectives  312 us (76%)
  waiting for transfers between devices  76.8 us (19%)
  between operations  15.5 us (4%)
  other arithmetic  8.11 us (2%)
    psum x1, blocking collectives, local(): lax.psum((local_squares[0], local_squares[1]), ('row', 'col'))  250 us
    psum x1, waiting for transfers between devices, local(): lax.psum(terms[0].astype(jnp.bfloat16), 'dp').astype(jnp.float32)  76.1 us
    psum x1, blocking collectives, column_totals(): lax.psum((jnp.sum(square_wi, axis=0), jnp.sum(square_wo, axis=0)), 'row')  45.7 us
    psum x1, blocking collectives, local(): lax.psum((jnp.sum(square_wi, axis=1), jnp.sum(square_wo, axis=1)), 'col')  16.8 us
  transfers between devices with their start and end apart: 1, of which 1 were waited for; matrix products, arithmetic and copies ran while one was open for 0% of the time, Pallas kernels for 0%

commit v1 on v0

--- a/solution.py
+++ b/solution.py
@@ -32,7 +32,8 @@
     raw_wi = total_wi / jnp.sqrt(row_new_wi[:, None] * col_new_wi[None, :])
     raw_wo = total_wo / jnp.sqrt(row_new_wo[:, None] * col_new_wo[None, :])
     local_squares = (jnp.sum(raw_wi * raw_wi), jnp.sum(raw_wo * raw_wo))
-    energy_wi, energy_wo = lax.psum((local_squares[0], local_squares[1]), ("row", "col"))
+    do_case = lambda x0, dev_axis, group_axis: lax.psum(lax.psum(x0, dev_axis), group_axis)
+    energy_wi, energy_wo = do_case((local_squares[0], local_squares[1]), "row", group_axis="col")
     update_wi = (raw_wi / jnp.maximum(1.0, jnp.sqrt(energy_wi / (D * FF)))).astype(jnp.bfloat16)
     update_wo = (raw_wo / jnp.maximum(1.0, jnp.sqrt(energy_wo / (D * FF)))).astype(jnp.bfloat16)
     return (update_wi, row_new_wi, col_new_wi, update_wo, row_new_wo, col_new_wo)

time: 413 us -> 205 us (0.50)
  the two profiles are of different devices: /device:TPU:64 before, /device:TPU:32 now
where the time goes in v1:
time: 205 us
  blocking collectives  104 us (51%)
  waiting for transfers between devices  77.1 us (38%)
  between operations  15.5 us (8%)
  other arithmetic  8.11 us (4%)
    psum x1, waiting for transfers between devices, local(): lax.psum(terms[0].astype(jnp.bfloat16), 'dp').astype(jnp.float32)  76.4 us
    psum x1, blocking collectives, column_totals(): lax.psum((jnp.sum(square_wi, axis=0), jnp.sum(square_wo, axis=0)), 'row')  45.8 us
    psum x1, blocking collectives, local(): lax.psum(x0, dev_axis)  24.2 us
    psum x1, blocking collectives, local(): lax.psum((jnp.sum(square_wi, axis=1), jnp.sum(square_wo, axis=1)), 'col')  18.4 us
    psum x1, blocking collectives, local(): lax.psum(lax.psum(x0, dev_axis), group_axis)  15.3 us
  transfers between devices with their start and end apart: 1, of which 1 were waited for; matrix products, arithmetic and copies ran while one was open for 0% of the time, Pallas kernels for 0%

profile of v1, /device:TPU:32, one launch (start us, length us, event | category | flops | bytes accessed | tf_op | source)
XLA Modules:
  0.0 204.5 jit_solution(1561780827785561097)
XLA Ops:
  7.2 0.0 all-reduce.7.cloned.1.call-start
  7.2 0.7 all-reduce.7.cloned.1.call-update
  7.9 76.4 %all-reduce.7.cloned.1.call-done = (bf16[256,2048]{1,0:T(8,128)(2,1)}, bf16[1024,512]{1,0:T(8,128)(2,1)}) async-done(((bf16[256,2048]{1,0:T(8,128)(2,1)}, bf16[1024,512]{1,0:T(8,128)(2,1)}), (bf16[256,2048]{1,0:T(8,128)(2,1)}, bf16[1024,512]{1,0:T(8,128)(2,1)})) %all-reduce.7.cloned.1.call-update) | async-done | bytes 2097168 | tf_op jit(solution)/shard_map/psum | solution.py:19
  84.4 1.8 fusion.5
  86.1 0.0 copy-done.1
  86.1 0.0 copy-start.8
  86.2 0.0 copy-start
  86.2 0.5 fusion.2
  86.7 18.4 %all-reduce.3 = (f32[256]{0:T(256)S(1)}, f32[1024]{0:T(1024)S(1)}) all-reduce(f32[256]{0:T(256)S(1)} %get-tuple-element.8, f32[1024]{0:T(1024)S(1)} %get-tuple-element.6), channel_id=1, replica_groups=mesh['dp'=4,'row'=16,'col'=8] {'col'}, use_global_device_ids=true, to_apply=%region_2.0 | all-reduce | flops 1280 | bytes 10240 | tf_op jit(solution)/shard_map/psum | solution.py:24
  105.1 0.0 copy-done.9
  105.1 0.0 copy-start.5
  105.1 0.0 copy-done.7
  105.2 0.0 copy-start.3
  105.2 45.8 %all-reduce.1 = (f32[2048]{0:T(1024)S(1)}, f32[512]{0:T(512)S(1)}) all-reduce(f32[2048]{0:T(1024)S(1)} %get-tuple-element.9, f32[512]{0:T(512)S(1)} %get-tuple-element.7), channel_id=1, replica_groups=mesh['dp'=4,'row'=16,'col'=8] {'row'}, use_global_device_ids=true, to_apply=%region_4.0 | all-reduce | flops 2560 | bytes 20480 | tf_op jit(solution)/shard_map/psum | solution.py:13
  150.9 0.0 copy-done.6
  150.9 0.0 copy-start.2
  150.9 1.5 multiply_reduce_fusion.1
  152.5 0.0 copy-done
  152.5 0.0 copy-start.4
  152.5 1.4 multiply_reduce_fusion
  153.9 24.2 %all-reduce = (f32[]{:T(128)}, f32[]{:T(128)}) all-reduce(f32[]{:T(128)} %multiply_reduce_fusion.1, f32[]{:T(128)} %multiply_reduce_fusion), channel_id=1, replica_groups=mesh['dp'=4,'row'=16,'col'=8] {'row'}, use_global_device_ids=true, to_apply=%region_6.0 | all-reduce | flops 2 | bytes 16 | tf_op jit(solution)/shard_map/psum | solution.py:35
  178.1 15.3 %all-reduce.2 = (f32[]{:T(128)}, f32[]{:T(128)}) all-reduce(f32[]{:T(128)} %get-tuple-element.10, f32[]{:T(128)} %get-tuple-element.11), channel_id=1, replica_groups=mesh['dp'=4,'row'=16,'col'=8] {'col'}, use_global_device_ids=true, to_apply=%region_7.0 | all-reduce | flops 2 | bytes 16 | tf_op jit(solution)/shard_map/psum | solution.py:35
  194.8 1.4 divide_convert_fusion.1
  196.2 1.4 divide_convert_fusion
  (13 shorter events, 0.0 us)
Async XLA Ops:
  7.2 77.2 %all-reduce.7.cloned.1.call-start = ((), (), s32[]{:S(2)}) async-start(), calls=%async_computation | async-start | bytes 4194304 | tf_op jit(solution)/shard_map/psum | solution.py:19
  84.3 1.8 copy-start.1
  84.3 20.7 %copy-start.9 = (f32[256]{0:T(256)S(1)}, f32[256]{0:T(256)}, u32[]{:S(2)}) copy-start(f32[256]{0:T(256)} %param.8) | copy-start | bytes 3076
  84.4 20.8 %copy-start.7 = (f32[1024]{0:T(1024)S(1)}, f32[1024]{0:T(1024)}, u32[]{:S(2)}) copy-start(f32[1024]{0:T(1024)} %param.10) | copy-start | bytes 12292
  84.4 66.6 %copy-start.6 = (f32[2048]{0:T(1024)S(1)}, f32[2048]{0:T(1024)}, u32[]{:S(2)}) copy-start(f32[2048]{0:T(1024)} %param.9) | copy-start | bytes 24580
  86.1 66.3 %copy-start.8 = (f32[512]{0:T(512)S(1)}, f32[512]{0:T(512)}, u32[]{:S(2)}) copy-start(f32[512]{0:T(512)} %param.11) | copy-start | bytes 6148
  86.2 66.3 %copy-start = (bf16[1024,512]{1,0:T(8,128)(2,1)S(1)}, bf16[1024,512]{1,0:T(8,128)(2,1)}, u32[]{:S(2)}) copy-start(bf16[1024,512]{1,0:T(8,128)(2,1)} %get-tuple-element.19) | copy-start | bytes 3145732
  105.1 89.7 %copy-start.5 = (f32[256]{0:T(256)}, f32[256]{0:T(256)S(1)}, u32[]{:S(2)}) copy-start(f32[256]{0:T(256)S(1)} %multiply_add_fusion.3) | copy-start | bytes 3076
  105.2 91.1 %copy-start.3 = (f32[1024]{0:T(1024)}, f32[1024]{0:T(1024)S(1)}, u32[]{:S(2)}) copy-start(f32[1024]{0:T(1024)S(1)} %multiply_add_fusion.1) | copy-start | bytes 12292
  150.9 43.9 %copy-start.2 = (f32[2048]{0:T(1024)}, f32[2048]{0:T(1024)S(1)}, u32[]{:S(2)}) copy-start(f32[2048]{0:T(1024)S(1)} %multiply_add_fusion) | copy-start | bytes 24580
  152.5 43.8 %copy-start.4 = (f32[512]{0:T(512)}, f32[512]{0:T(512)S(1)}, u32[]{:S(2)}) copy-start(f32[512]{0:T(512)S(1)} %multiply_add_fusion.2) | copy-start | bytes 6148
Sparse Core Ops, SparseCore 0:
  10.4 73.8 all-reduce.6
